TPU v7x, 128 devices: a whole 4x4x4 slice. The times are simulated.
128 devices in a mesh: img: 8 (over x, core), txt: 16 (over y, z).
Axes of the slice: x: 4, y: 4, z: 4, core: 2. Of those that a mesh axis runs over, the one named last changes fastest.
Arguments:
- image_feat: float32 [16384, 1280], P(('img', 'txt')), may hold values from -1 to 1
- text_feat: float32 [16384, 1280], P(('txt', 'img')), may hold values from -1 to 1
- logit_temp: float32 [], replicated, may hold values from 4.4 to 4.6
Outputs:
- mean_loss: float32 [], replicated
- grad_image: float32 [16384, 1280], P(('img', 'txt'))
- grad_text: float32 [16384, 1280], P(('txt', 'img'))
- temp_grad: float32 [], replicated
All inputs are finite; a program needn't handle non-finite values.
Results may differ from a plain program's by a relative error of at most 0.013.
Values may be sent and summed in bfloat16 or wider, within the bound.
A program may use at most 128 MiB of HBM per device.

v0:
```python
import functools

import jax
import jax.numpy as jnp
from jax import lax
from jax.experimental import pallas as pl
from jax.experimental.pallas import tpu as pltpu
from jax.sharding import PartitionSpec as P

PLACE = {(0, 0): 0, (0, 1): 1, (1, 0): 2, (3, 0): 3, (1, 1): 4, (3, 1): 5, (2, 0): 6, (2, 1): 7}
BLOCK = 128
HALF = 64
QUARTER = 32
WIDTH = 1280
PAIRS = 16384
GROUP = 256
LOG2E = 1.4426950408889634
LN2 = 0.6931471805599453
HIGH_SHIFT = 33.0
LOW_SHIFT = 86.0
LOW_CAP = 20.0
HIGH_LEAST = 2.0**-62
F32 = jnp.float32
BF16 = jnp.bfloat16


def exp_of(temp):
    return jnp.max(jnp.exp(jnp.full((8, 128), temp, F32)))


def mod4(v):
    return lax.rem(v + 4, 4)


class Copies:
    def __init__(self, send_sems, recv_sems):
        self.send_sems, self.recv_sems = send_sems, recv_sems
        self.table = {}

    def start(self, name, src, dst, device):
        index = len(self.table)
        copy = pltpu.make_async_remote_copy(
            src_ref=src,
            dst_ref=dst,
            send_sem=self.send_sems.at[index],
            recv_sem=self.recv_sems.at[index],
            device_id=device,
            device_id_type=pl.DeviceIdType.MESH,
        )
        copy.start()
        self.table[name] = copy

    def arrived(self, name):
        self.table[name].wait_recv()

    def finish(self):
        for copy in self.table.values():
            copy.wait_send()


def kernel(
    temp_ref,
    image_hbm,
    text_hbm,
    totals_ref,
    sum_image_hbm,
    sum_text_hbm,
    image_ref,
    text_ref,
    img,
    txt,
    dots,
    wts,
    row1,
    row2,
    col1,
    col2,
    row_shift,
    col_shift,
    diagonals,
    extra,
    img_stats,
    txt_stats,
    sums_a,
    sums_b,
    img_acc,
    txt_acc,
    img_out,
    txt_out,
    core_out,
    img_in,
    txt_in,
    core_in,
    send_sems,
    recv_sems,
    local_sems,
):
    img_index = lax.axis_index("img")
    txt_index = lax.axis_index("txt")
    x, core = img_index // 2, lax.rem(img_index, 2)
    y, z = txt_index // 4, lax.rem(txt_index, 4)
    odd = lax.rem(z, 2)
    z_img = z + 1 - 2 * odd
    z_txt = mod4(z - 1 + 2 * odd)

    def img_peer(r, q):
        return (img_index, mod4(y + r) * 4 + (z_img if q else z))

    def txt_peer(r, q, c=0):
        return (
            mod4(x + r) * 2 + (1 - core if c else core),
            y * 4 + (z_txt if q else z),
        )

    img_offsets = [(r, q) for r in range(4) for q in range(2) if (r, q) != (0, 0)]
    txt_offsets = [
        (r, q, c) for r in range(4) for q in range(2) for c in range(2) if (r, q, c) != (0, 0, 0)
    ]
    load_image = pltpu.make_async_copy(image_hbm, image_ref, local_sems.at[0])
    load_text = pltpu.make_async_copy(text_hbm, text_ref, local_sems.at[1])
    load_image.start()
    load_text.start()
    barrier = pltpu.get_barrier_semaphore()
    for offset in img_offsets:
        pl.semaphore_signal(barrier, inc=1, device_id=img_peer(*offset), device_id_type=pl.DeviceIdType.MESH)
    for offset in txt_offsets:
        pl.semaphore_signal(barrier, inc=1, device_id=txt_peer(*offset), device_id_type=pl.DeviceIdType.MESH)

    scale = exp_of(temp_ref[0, 0])
    slope = scale * LOG2E

    def inverse_of(rows):
        return lax.rsqrt(jnp.sum(rows * rows, axis=1, keepdims=True) + 1e-06)

    def normalize(source, target):
        for first in range(0, BLOCK, 32):
            rows = source[first : first + 32, :]
            target[first : first + 32, :] = (rows * inverse_of(rows)).astype(BF16)

    load_image.wait()
    normalize(image_ref, img)
    pl.semaphore_wait(barrier, len(img_offsets) + len(txt_offsets))

    copies = Copies(send_sems, recv_sems)

    def half(place, part):
        return pl.ds(place * BLOCK + part * HALF, HALF)

    sides = (("i", img, img_peer), ("t", txt, txt_peer))

    def push(side, name, place, first, count, to_place, r, q):
        label, rows, peer = side
        copies.start(
            label + name + str(first),
            rows.at[pl.ds(place * BLOCK + first, count)],
            rows.at[pl.ds(to_place * BLOCK + first, count)],
            peer(r, q),
        )

    def to_core(place, first, count):
        copies.start(
            "c%d_%d" % (place, first),
            txt.at[pl.ds(place * BLOCK + first, count)],
            txt.at[pl.ds((8 + place) * BLOCK + first, count)],
            txt_peer(0, 0, 1),
        )

    def push_own(side):
        push(side, "up", 0, 0, QUARTER, PLACE[3, 0], 1, 0)
        push(side, "down", 0, 64, QUARTER, PLACE[1, 0], 3, 0)
        push(side, "z", 0, 0, HALF, PLACE[0, 1], 0, 1)
        push(side, "up", 0, 32, QUARTER, PLACE[3, 0], 1, 0)
        push(side, "down", 0, 96, QUARTER, PLACE[1, 0], 3, 0)
        push(side, "up", 0, 64, HALF, PLACE[3, 0], 1, 0)
        push(side, "down", 0, 0, HALF, PLACE[1, 0], 3, 0)
        push(side, "z", 0, 64, HALF, PLACE[0, 1], 0, 1)

    push_own(sides[0])
    load_text.wait()
    normalize(text_ref, txt)
    push_own(sides[1])
    to_core(0, 0, BLOCK)

    row1[...] = jnp.zeros_like(row1)
    row2[...] = jnp.zeros_like(row2)
    col1[...] = jnp.zeros_like(col1)
    col2[...] = jnp.zeros_like(col2)

    def forward(row, row_count, column, column_count):
        cols = pl.ds(column, column_count)
        product = lax.dot_general(
            img[pl.ds(row, row_count), :],
            txt[cols, :],
            (((1,), (1,)), ((), ())),
            preferred_element_type=F32,
        )
        dots[pl.ds(row, row_count), cols] = product * slope

        for first in range(row, row + row_count, 32):
            part = pl.ds(first, 32)
            add1 = jnp.zeros((32, 128), F32)
            add2 = jnp.zeros((32, 128), F32)
            for lane in range(column, column + column_count, 128):
                block_cols = pl.ds(lane, 128)
                score = dots[part, block_cols]
                mass1 = jnp.exp2(score - HIGH_SHIFT)
                mass2 = jnp.exp2(jnp.minimum(score, LOW_CAP) + LOW_SHIFT)
                add1 = add1 + mass1
                add2 = add2 + mass2
                col1[:, block_cols] += jnp.sum(mass1.reshape(32 // 8, 8, 128), axis=0)
                col2[:, block_cols] += jnp.sum(mass2.reshape(32 // 8, 8, 128), axis=0)
            row1[part, :] += add1
            row2[part, :] += add2

    def wait_core(*names):
        for name in names:
            copies.arrived("c" + name)

    def take(name, first):
        for side in sides:
            copies.arrived(side[0] + name + str(first))

    for first in (0, 32):
        for side in sides:
            copies.arrived(side[0] + "up" + str(first))
            push(side, "up2_", PLACE[3, 0], first, QUARTER, PLACE[2, 0], 1, 0)
            copies.arrived(side[0] + "down" + str(64 + first))
            push(side, "down2_", PLACE[1, 0], 64 + first, QUARTER, PLACE[2, 0], 3, 0)
    to_core(PLACE[3, 0], 0, HALF)
    to_core(PLACE[1, 0], 64, HALF)
    take("up", 64)
    take("down", 0)
    to_core(PLACE[3, 0], 64, HALF)
    to_core(PLACE[1, 0], 0, HALF)
    for first in (0, 64):
        for side in sides:
            copies.arrived(side[0] + "z" + str(first))
            push(side, "zup", PLACE[0, 1], first, HALF, PLACE[3, 1], 1, 0)
            push(side, "zdown", PLACE[0, 1], first, HALF, PLACE[1, 1], 3, 0)
    to_core(PLACE[0, 1], 0, BLOCK)
    for first in (0, 32):
        for side in sides:
            copies.arrived(side[0] + "up2_" + str(first))
            push(side, "up2z", PLACE[2, 0], first, QUARTER, PLACE[2, 1], 0, 1)
            copies.arrived(side[0] + "down2_" + str(64 + first))
            push(side, "down2z", PLACE[2, 0], 64 + first, QUARTER, PLACE[2, 1], 0, 1)
    to_core(PLACE[2, 0], 0, BLOCK)
    forward(0, 512, 0, 512)
    wait_core("0_0", "1_0", "2_0", "2_64", "3_0", "3_64", "6_0")
    forward(0, 512, 1024, 512)
    take("zup", 0)
    take("zdown", 0)
    to_core(PLACE[3, 1], 0, HALF)
    to_core(PLACE[1, 1], 0, HALF)
    forward(768, 128, 0, 512)
    forward(768, 128, 1024, 512)
    take("up2z", 0)
    take("down2z", 64)
    take("up2z", 32)
    take("down2z", 96)
    to_core(PLACE[2, 1], 0, BLOCK)
    take("zup", 64)
    take("zdown", 64)
    to_core(PLACE[3, 1], 64, HALF)
    to_core(PLACE[1, 1], 64, HALF)
    forward(512, 256, 0, 1024)
    forward(896, 128, 0, 512)
    wait_core("7_0", "4_0", "5_0", "4_64", "5_64")
    forward(0, 512, 512, 512)
    forward(768, 256, 512, 512)
    forward(512, 256, 1024, 1024)
    forward(896, 128, 1024, 512)
    forward(0, 512, 1536, 512)
    forward(768, 256, 1536, 512)

    def img_order(r, q):
        return mod4(y + r) * 2 + (1 - odd if q else odd)

    def txt_order(r, q, c):
        return (mod4(x + r) * 2 + (odd if q else 1 - odd)) * 2 + (1 - core if c else core)

    for (r, q), place in PLACE.items():
        for c in range(2):
            cols = pl.ds((8 * c + place) * BLOCK, BLOCK)
            where = txt_order(r, q, c)
            txt_stats[0, pl.ds(where, 1), :] = jnp.sum(col1[:, cols], axis=0, keepdims=True)
            txt_stats[0, pl.ds(16 + where, 1), :] = jnp.sum(col2[:, cols], axis=0, keepdims=True)
    for r, q, c in txt_offsets:
        index = 8 * c + PLACE[(4 - r) % 4, q]
        copies.start("st%d" % index, txt_stats.at[0], txt_stats.at[index], txt_peer(r, q, c))
    for (r, q), place in PLACE.items():
        rows = pl.ds(place * BLOCK, BLOCK)
        where = img_order(r, q)
        img_stats[0, pl.ds(where, 1), :] = jnp.sum(row1[rows, :].T, axis=0, keepdims=True)
        img_stats[0, pl.ds(8 + where, 1), :] = jnp.sum(row2[rows, :].T, axis=0, keepdims=True)
    for r, q in img_offsets:
        index = PLACE[(4 - r) % 4, q]
        copies.start("si%d" % index, img_stats.at[0], img_stats.at[index], img_peer(r, q))

    eye = lax.broadcasted_iota(jnp.int32, (BLOCK, BLOCK), 0) == lax.broadcasted_iota(jnp.int32, (BLOCK, BLOCK), 1)

    def on_diagonal(place, body, wanted=lambda group: 1):
        r, q = [key for key in PLACE if PLACE[key] == place][0]
        y_row, z_row = mod4(y + r), (z_img if q else z)
        x_text, z_text, core_text = lax.rem(y_row, 2) * 2 + z_row // 2, 2 * core + y_row // 2, lax.rem(z_row, 2)
        near = jnp.where(z_text == z, 1, 0)
        far = jnp.where(z_text == z_txt, 1, 0)
        ring = mod4(x_text - x)
        place_text = jnp.where(
            ring == 0, far, jnp.where(ring == 1, 2 + 2 * far, jnp.where(ring == 2, 6 + far, 3 + 2 * far))
        )
        place_text = place_text + 8 * jnp.where(core_text == core, 0, 1)

        @pl.when(jnp.where(x == y, near + far, 0) * wanted(place_text // 2) == 1)
        def _():
            body(pl.ds(place * BLOCK, BLOCK), pl.ds(pl.multiple_of(place_text * BLOCK, BLOCK), BLOCK))

    for place in range(8):

        def set_aside(rows, cols, place=place):
            scores = dots[rows, cols]
            diagonals[place] = scores
            dots[rows, cols] = jnp.where(eye, -10000.0, scores)

        on_diagonal(place, set_aside)

    def log_sum(high, low):
        return jnp.where(
            high >= HIGH_LEAST,
            jnp.log(high) * LOG2E + HIGH_SHIFT,
            jnp.log(jnp.maximum(low, 1e-37)) * LOG2E - LOW_SHIFT,
        )

    img_total = img_stats[0]
    for index in range(1, 8):
        copies.arrived("si%d" % index)
        img_total = img_total + img_stats[index]
    row_lse = log_sum(img_total[:8], img_total[8:])
    row1[0:8, :] = row_lse
    own_lse = row1[pl.ds(img_order(0, 0), 1), :]
    for (r, q), place in PLACE.items():
        one = row1[pl.ds(img_order(r, q), 1), :]
        row_shift[pl.ds(place * BLOCK, BLOCK), :] = jnp.broadcast_to(one + 1.0, (BLOCK, BLOCK)).T
    txt_total = txt_stats[0]
    for index in range(1, 16):
        copies.arrived("st%d" % index)
        txt_total = txt_total + txt_stats[index]
    col_lse = log_sum(txt_total[:16], txt_total[16:])
    row2[0:16, :] = col_lse
    own_lse = own_lse + row2[pl.ds(txt_order(0, 0, 0), 1), :]
    for (r, q), place in PLACE.items():
        for c in range(2):
            one = row2[pl.ds(txt_order(r, q, c), 1), :]
            col_shift[:, pl.ds((8 * c + place) * BLOCK, BLOCK)] = one + 1.0

    extra[...] = jnp.zeros_like(extra)
    heats = [jnp.zeros((16, 128), F32)] * 4

    def weigh(places, blocks):
        for place in places:
            for first in range(place * BLOCK, place * BLOCK + BLOCK, 16):
                part = pl.ds(first, 16)
                shift = row_shift[part, :]
                for block in blocks:
                    cols = pl.ds(block * BLOCK, BLOCK)
                    score = dots[part, cols]
                    weight = jnp.exp2(score - shift) + jnp.exp2(score - col_shift[:, cols])
                    heats[block % 4] = heats[block % 4] + weight * score
                    wts[part, cols] = weight.astype(BF16)

    def put_back(places, wanted):
        def body(place, rows, cols):
            scores = diagonals[place]
            weight = jnp.exp2(scores - row_shift[rows, :]) + jnp.exp2(scores - col_shift[:, cols])
            weight = jnp.where(eye, weight - 1.0, weight)
            wts[rows, cols] = weight.astype(BF16)
            extra[0:1, :] += jnp.sum(jnp.where(eye, scores, 0.0), axis=0, keepdims=True)
            extra[1:2, :] += jnp.sum(jnp.where(eye, weight * scores, 0.0), axis=0, keepdims=True)

        for place in places:
            on_diagonal(place, functools.partial(body, place), wanted)

    def block(place):
        return pl.ds(place * BLOCK, BLOCK)

    def rows_of(group):
        return pl.ds(group * GROUP, GROUP)

    def image_term(group):
        return jnp.dot(wts[rows_of(group), :], txt[...], preferred_element_type=F32)

    def text_term(group):
        return lax.dot_general(
            wts[:, rows_of(group)], img[...], (((0,), (0,)), ((), ())), preferred_element_type=F32
        )

    def core_step(group):
        rows = rows_of(group)
        core_out[rows, :] = text_term(4 + group).astype(BF16)
        copies.start("k%d" % group, core_out.at[rows], core_in.at[rows], txt_peer(0, 0, 1))

    def text_group(group):
        term = text_term(group)
        copies.arrived("k%d" % group)
        return term + core_in[rows_of(group), :].astype(F32)

    trees = (("i", img_acc, img_out, img_in, img_peer), ("t", txt_acc, txt_out, txt_in, txt_peer))

    def group_term(tree, group):
        return image_term(group) if tree[0] == "i" else text_group(group)

    def send(tree, name, place, first, count, to_place, r, q):
        label, acc, out, landing, peer = tree
        rows = pl.ds(place * BLOCK + first, count)
        copies.start(label + name, out.at[rows], landing.at[pl.ds(to_place * BLOCK + first, count)], peer(r, q))

    def lower(tree, place, first, count, slots):
        label, acc, out, landing, peer = tree
        rows = pl.ds(place * BLOCK + first, count)
        total = acc[rows, :]
        for slot in slots:
            total = total + landing[pl.ds(slot * BLOCK + first, count), :].astype(F32)
        out[rows, :] = total.astype(BF16)

    def ring_step(tree):
        tree[2][rows_of(2), :] = group_term(tree, 2).astype(BF16)
        for first in (0, HALF):
            send(tree, "zup_g%d" % first, 4, first, HALF, 1, 1, 0)
            send(tree, "zdown_g%d" % first, 5, first, HALF, 2, 3, 0)

    def far_step(tree):
        term = group_term(tree, 3)
        tree[1][block(6), :] = term[:BLOCK]
        tree[2][block(7), :] = term[BLOCK:].astype(BF16)
        for first in (0, 64, 32, 96):
            send(tree, "far_g%d" % first, 7, first, QUARTER, 0, 0, 1)

    def turn_step(tree, first):
        copies.arrived(tree[0] + "far_g%d" % first)
        lower(tree, 6, first, QUARTER, (0,))
        send(tree, "down2_g%d" % first, 6, first, QUARTER, 3, 3, 0)
        copies.arrived(tree[0] + "far_g%d" % (64 + first))
        lower(tree, 6, 64 + first, QUARTER, (0,))
        send(tree, "up2_g%d" % first, 6, 64 + first, QUARTER, 3, 1, 0)

    def free_step(tree):
        term = group_term(tree, 1)
        tree[2][half(2, 0), :] = term[:HALF].astype(BF16)
        tree[1][half(2, 1), :] = term[HALF : 2 * HALF]
        tree[1][half(3, 0), :] = term[2 * HALF : 3 * HALF]
        tree[2][half(3, 1), :] = term[3 * HALF :].astype(BF16)
        send(tree, "up_free", 2, 0, HALF, 4, 1, 0)
        send(tree, "down_free", 3, HALF, HALF, 5, 3, 0)

    def own_step(tree):
        tree[1][rows_of(0), :] = group_term(tree, 0)

    def pair_step(tree, first):
        copies.arrived(tree[0] + "zup_g%d" % first)
        copies.arrived(tree[0] + "zdown_g%d" % first)
        lower(tree, 1, first, HALF, (1, 2))
        send(tree, "z_g%d" % first, 1, first, HALF, 6, 0, 1)

    def last_step(tree, first):
        copies.arrived(tree[0] + "up2_g%d" % first)
        lower(tree, 2, 64 + first, QUARTER, (3,))
        send(tree, "up_last%d" % first, 2, 64 + first, QUARTER, 4, 1, 0)
        copies.arrived(tree[0] + "down2_g%d" % first)
        lower(tree, 3, first, QUARTER, (3,))
        send(tree, "down_last%d" % first, 3, first, QUARTER, 5, 3, 0)

    image_tree, text_tree = trees
    weigh(range(8), range(16))
    put_back(range(8), lambda group: 1)
    sums_a[0, 0:1, :] = own_lse - 2.0 * extra[0:1, :]
    sums_a[0, 1:2, :] = jnp.sum(heats[0] + heats[1] + heats[2] + heats[3], axis=0, keepdims=True) + extra[1:2, :]
    sums_a[0, 2:8, :] = jnp.zeros((6, 128), F32)
    for r, q in img_offsets:
        index = PLACE[(4 - r) % 4, q]
        copies.start("ai%d" % index, sums_a.at[0], sums_a.at[index], img_peer(r, q))

    core_step(2)
    ring_step(image_tree)
    ring_step(text_tree)
    core_step(3)
    far_step(image_tree)
    far_step(text_tree)
    core_step(1)
    free_step(image_tree)
    free_step(text_tree)
    for index in range(1, 8):
        copies.arrived("ai%d" % index)
    total = sums_a[0]
    for index in range(1, 8):
        total = total + sums_a[index]
    sums_b[0] = total
    for r, q, c in txt_offsets:
        index = 8 * c + PLACE[(4 - r) % 4, q]
        copies.start("at%d" % index, sums_b.at[0], sums_b.at[index], txt_peer(r, q, c))
    core_step(0)
    own_step(image_tree)
    turn_step(image_tree, 0)
    own_step(text_tree)
    turn_step(text_tree, 0)
    pair_step(image_tree, 0)
    pair_step(image_tree, HALF)
    turn_step(image_tree, QUARTER)
    pair_step(text_tree, 0)
    pair_step(text_tree, HALF)
    turn_step(text_tree, QUARTER)
    for first in (0, QUARTER):
        for tree in trees:
            last_step(tree, first)
    for index in range(1, 16):
        copies.arrived("at%d" % index)
    total = sums_b[0]
    for index in range(1, 16):
        total = total + sums_b[index]
    totals_ref[...] = total
    stores = []
    for tree, source, result in ((image_tree, image_ref, sum_image_hbm), (text_tree, text_ref, sum_text_hbm)):
        label, acc, out, landing, peer = tree
        for name in ("up_free", "down_free", "z_g0", "z_g64", "up_last0", "down_last0", "up_last32", "down_last32"):
            copies.arrived(label + name)
        grad = acc[block(0), :]
        for slot in (4, 5, 6):
            grad = grad + landing[block(slot), :].astype(F32)
        source[...] = grad
        stores.append(pltpu.make_async_copy(source, result, local_sems.at[2 + len(stores)]))
        stores[-1].start()
    copies.finish()
    for store in stores:
        store.wait()


def finalize(
    temp_ref,
    totals_ref,
    image_ref,
    text_ref,
    sum_image_ref,
    sum_text_ref,
    loss_ref,
    grad_image_ref,
    grad_text_ref,
    temp_grad_ref,
):
    scale = exp_of(temp_ref[0, 0])
    for source, total, result in (
        (image_ref, sum_image_ref, grad_image_ref),
        (text_ref, sum_text_ref, grad_text_ref),
    ):
        rows = source[...]
        inverse = lax.rsqrt(jnp.sum(rows * rows, axis=1, keepdims=True) + 1e-06)
        grad = total[...] * scale
        unit = rows * inverse
        result[...] = inverse * (grad - unit * jnp.sum(unit * grad, axis=1, keepdims=True))
    totals = totals_ref[...]
    loss_ref[0, 0] = jnp.sum(totals[0:1, :]) * (LN2 / (2.0 * PAIRS))
    temp_grad_ref[0, 0] = jnp.sum(totals[1:2, :]) * (LN2 / PAIRS)


def on_device(image_feat, text_feat, logit_temp):
    logit_temp = logit_temp.reshape(1, 1)
    smem = pl.BlockSpec(memory_space=pltpu.SMEM)
    anywhere = pl.BlockSpec(memory_space=pl.ANY)
    one = jax.ShapeDtypeStruct((1, 1), F32)
    shape = jax.ShapeDtypeStruct((BLOCK, WIDTH), F32)
    totals, sum_image, sum_text = pl.pallas_call(
        kernel,
        out_shape=(jax.ShapeDtypeStruct((8, 128), F32), shape, shape),
        in_specs=[smem, anywhere, anywhere],
        out_specs=(pl.BlockSpec(memory_space=pltpu.VMEM), anywhere, anywhere),
        scratch_shapes=[
            pltpu.VMEM((BLOCK, WIDTH), F32),
            pltpu.VMEM((BLOCK, WIDTH), F32),
            pltpu.VMEM((1024, WIDTH), BF16),
            pltpu.VMEM((2048, WIDTH), BF16),
            pltpu.VMEM((1024, 2048), F32),
            pltpu.VMEM((1024, 2048), BF16),
            pltpu.VMEM((1024, 128), F32),
            pltpu.VMEM((1024, 128), F32),
            pltpu.VMEM((8, 2048), F32),
            pltpu.VMEM((8, 2048), F32),
            pltpu.VMEM((1024, 128), F32),
            pltpu.VMEM((1, 2048), F32),
            pltpu.VMEM((8, BLOCK, BLOCK), F32),
            pltpu.VMEM((8, 128), F32),
            pltpu.VMEM((8, 16, 128), F32),
            pltpu.VMEM((16, 32, 128), F32),
            pltpu.VMEM((8, 8, 128), F32),
            pltpu.VMEM((16, 8, 128), F32),
            pltpu.VMEM((1024, WIDTH), F32),
            pltpu.VMEM((1024, WIDTH), F32),
            pltpu.VMEM((1024, WIDTH), BF16),
            pltpu.VMEM((1024, WIDTH), BF16),
            pltpu.VMEM((1024, WIDTH), BF16),
            pltpu.VMEM((7 * BLOCK, WIDTH), BF16),
            pltpu.VMEM((7 * BLOCK, WIDTH), BF16),
            pltpu.VMEM((1024, WIDTH), BF16),
            pltpu.SemaphoreType.DMA((160,)),
            pltpu.SemaphoreType.DMA((160,)),
            pltpu.SemaphoreType.DMA((4,)),
        ],
        compiler_params=pltpu.CompilerParams(
            collective_id=0, has_side_effects=True, vmem_limit_bytes=60 * 2**20
        ),
        cost_estimate=pl.CostEstimate(flops=16106127360, bytes_accessed=2621440, transcendentals=8388608),
    )(logit_temp, image_feat, text_feat)
    step_rows = 64
    rows = pl.BlockSpec((step_rows, WIDTH), lambda i: (i, 0))
    mean_loss, grad_image, grad_text, temp_grad = pl.pallas_call(
        finalize,
        grid=(BLOCK // step_rows,),
        out_shape=(one, shape, shape, one),
        in_specs=[smem, pl.BlockSpec((8, 128), lambda i: (0, 0)), rows, rows, rows, rows],
        out_specs=(smem, rows, rows, smem),
    )(logit_temp, totals, image_feat, text_feat, sum_image, sum_text)
    return (mean_loss[0, 0], grad_image, grad_text, temp_grad[0, 0])


def solution(mesh):
    in_specs = (P(("img", "txt"), None), P(("txt", "img"), None), P())
    out_specs = (P(), P(("img", "txt"), None), P(("txt", "img"), None), P())
    return jax.shard_map(
        on_device, mesh=mesh, in_specs=in_specs, out_specs=out_specs, check_vma=False
    )
```

profile of v0, /device:TPU:1, one launch (start us, length us, event | category | flops | bytes accessed | tf_op | source)
XLA Modules:
  0.0 78.6 jit_solution(8589661157313376548)
XLA Ops:
  1.3 74.5 %shard_map.66 = (f32[8,128]{1,0:T(8,128)}, f32[128,1280]{1,0:T(8,128)}, f32[128,1280]{1,0:T(8,128)}) custom-call(f32[1,1]{1,0:T(1,128)} %bitcast.3.temp_ref, f32[128,1280]{1,0:T(8,128)} %image_ref.1, f32[128,1280]{1,0:T(8,128)} %text_ref.1), custom_call_target="tpu_custom_call" | custom-call | flops 16106127360 | bytes 2621440 | tf_op jit(solution)/shard_map/pallas_call | solution.py:569
  75.8 2.8 %shard_map.67 = (f32[1,1]{1,0:T(1,128)}, f32[128,1280]{1,0:T(8,128)}, f32[128,1280]{1,0:T(8,128)}, f32[1,1]{1,0:T(1,128)}) custom-call(f32[1,1]{1,0:T(1,128)} %bitcast.4.temp_ref, f32[8,128]{1,0:T(8,128)} %get-tuple-element.11.totals_ref, f32[128,1280]{1,0:T(8,128)} %image_ref.1, f32[128,1280]{1,0:T(8,128)} %text_ref.1, ...), custom_call_target="tpu_custom_call" | custom-call | tf_op jit(solution)/shard_map/pallas_call | solution.py:612
where the time goes:
time: 78.8 us; the launch traced here: 78.6 us
  Pallas kernels  77.3 us (98%)
  between operations  1.29 us (2%)
    pallas_call x1, Pallas kernels, on_device(): pl.pallas_call(kernel, out_shape=(jax.ShapeDtypeStruct((8, 128), F32), sh...  74.5 us
    pallas_call x1, Pallas kernels, on_device(): pl.pallas_call(finalize, grid=(BLOCK // step_rows,), out_shape=(one, shap...  2.77 us

commit v1 on v0

--- a/solution.py
+++ b/solution.py
@@ -36,6 +36,7 @@
     def __init__(self, send_sems, recv_sems):
         self.send_sems, self.recv_sems = send_sems, recv_sems
         self.table = {}
+        self.settled = 0
 
     def start(self, name, src, dst, device):
         index = len(self.table)
@@ -53,9 +54,10 @@
     def arrived(self, name):
         self.table[name].wait_recv()
 
-    def finish(self):
-        for copy in self.table.values():
+    def settle(self, count):
+        for copy in list(self.table.values())[self.settled : count]:
             copy.wait_send()
+        self.settled = count
 
 
 def kernel(
@@ -265,13 +267,15 @@
     to_core(PLACE[1, 1], 64, HALF)
     forward(512, 256, 0, 1024)
     forward(896, 128, 0, 512)
-    wait_core("7_0", "4_0", "5_0", "4_64", "5_64")
     forward(0, 512, 512, 512)
     forward(768, 256, 512, 512)
+    wait_core("7_0", "4_0", "5_0", "4_64", "5_64")
     forward(512, 256, 1024, 1024)
     forward(896, 128, 1024, 512)
     forward(0, 512, 1536, 512)
     forward(768, 256, 1536, 512)
+
+    gather_count = len(copies.table)
 
     def img_order(r, q):
         return mod4(y + r) * 2 + (1 - odd if q else odd)
@@ -331,6 +335,7 @@
             jnp.log(jnp.maximum(low, 1e-37)) * LOG2E - LOW_SHIFT,
         )
 
+    copies.settle(gather_count)
     img_total = img_stats[0]
     for index in range(1, 8):
         copies.arrived("si%d" % index)
@@ -488,6 +493,7 @@
     core_step(1)
     free_step(image_tree)
     free_step(text_tree)
+    far_count = len(copies.table)
     for index in range(1, 8):
         copies.arrived("ai%d" % index)
     total = sums_a[0]
@@ -508,9 +514,11 @@
     pair_step(text_tree, 0)
     pair_step(text_tree, HALF)
     turn_step(text_tree, QUARTER)
-    for first in (0, QUARTER):
-        for tree in trees:
-            last_step(tree, first)
+    for tree in trees:
+        last_step(tree, 0)
+    copies.settle(far_count)
+    for tree in trees:
+        last_step(tree, QUARTER)
     for index in range(1, 16):
         copies.arrived("at%d" % index)
     total = sums_b[0]
@@ -528,7 +536,7 @@
         source[...] = grad
         stores.append(pltpu.make_async_copy(source, result, local_sems.at[2 + len(stores)]))
         stores[-1].start()
-    copies.finish()
+    copies.settle(len(copies.table))
     for store in stores:
         store.wait()
 

time: 78.8 us -> 77.6 us (0.985)
  Pallas kernels: 77.3 us -> 76.1 us
    pallas_call x1, Pallas kernels: 74.5 us -> 73.3 us  [on_device(): pl.pallas_call(kernel, out_shape=(jax.ShapeDtypeStruct((8, 128), F32), sh...]
where the time goes in v1:
time: 77.6 us; the launch traced here: 77.4 us
  Pallas kernels  76.1 us (98%)
  between operations  1.29 us (2%)
    pallas_call x1, Pallas kernels, on_device(): pl.pallas_call(kernel, out_shape=(jax.ShapeDtypeStruct((8, 128), F32), sh...  73.3 us
    pallas_call x1, Pallas kernels, on_device(): pl.pallas_call(finalize, grid=(BLOCK // step_rows,), out_shape=(one, shap...  2.77 us

profile of v1, /device:TPU:1, one launch (start us, length us, event | category | flops | bytes accessed | tf_op | source)
XLA Modules:
  0.0 77.4 jit_solution(4423769593318983658)
XLA Ops:
  1.3 73.3 %shard_map.66 = (f32[8,128]{1,0:T(8,128)}, f32[128,1280]{1,0:T(8,128)}, f32[128,1280]{1,0:T(8,128)}) custom-call(f32[1,1]{1,0:T(1,128)} %bitcast.3.temp_ref, f32[128,1280]{1,0:T(8,128)} %image_ref.1, f32[128,1280]{1,0:T(8,128)} %text_ref.1), custom_call_target="tpu_custom_call" | custom-call | flops 16106127360 | bytes 2621440 | tf_op jit(solution)/shard_map/pallas_call | solution.py:577
  74.6 2.8 %shard_map.67 = (f32[1,1]{1,0:T(1,128)}, f32[128,1280]{1,0:T(8,128)}, f32[128,1280]{1,0:T(8,128)}, f32[1,1]{1,0:T(1,128)}) custom-call(f32[1,1]{1,0:T(1,128)} %bitcast.4.temp_ref, f32[8,128]{1,0:T(8,128)} %get-tuple-element.11.totals_ref, f32[128,1280]{1,0:T(8,128)} %image_ref.1, f32[128,1280]{1,0:T(8,128)} %text_ref.1, ...), custom_call_target="tpu_custom_call" | custom-call | tf_op jit(solution)/shard_map/pallas_call | solution.py:620

commit v2 on v1

--- a/solution.py
+++ b/solution.py
@@ -228,6 +228,9 @@
             push(side, "up2_", PLACE[3, 0], first, QUARTER, PLACE[2, 0], 1, 0)
             copies.arrived(side[0] + "down" + str(64 + first))
             push(side, "down2_", PLACE[1, 0], 64 + first, QUARTER, PLACE[2, 0], 3, 0)
+            if first == 32:
+                push(side, "zup", PLACE[3, 0], 32, 16, PLACE[3, 1], 0, 1)
+                push(side, "zdown", PLACE[1, 0], 96, 16, PLACE[1, 1], 0, 1)
     to_core(PLACE[3, 0], 0, HALF)
     to_core(PLACE[1, 0], 64, HALF)
     take("up", 64)
@@ -237,8 +240,13 @@
     for first in (0, 64):
         for side in sides:
             copies.arrived(side[0] + "z" + str(first))
-            push(side, "zup", PLACE[0, 1], first, HALF, PLACE[3, 1], 1, 0)
-            push(side, "zdown", PLACE[0, 1], first, HALF, PLACE[1, 1], 3, 0)
+            if first == 0:
+                push(side, "zup", PLACE[0, 1], 0, 32, PLACE[3, 1], 1, 0)
+                push(side, "zdown", PLACE[0, 1], 0, 64, PLACE[1, 1], 3, 0)
+            else:
+                push(side, "zup", PLACE[0, 1], 48, 80, PLACE[3, 1], 1, 0)
+                push(side, "zdown", PLACE[0, 1], 64, 32, PLACE[1, 1], 3, 0)
+                push(side, "zdown", PLACE[0, 1], 112, 16, PLACE[1, 1], 3, 0)
     to_core(PLACE[0, 1], 0, BLOCK)
     for first in (0, 32):
         for side in sides:
@@ -252,7 +260,9 @@
     forward(0, 512, 1024, 512)
     take("zup", 0)
     take("zdown", 0)
-    to_core(PLACE[3, 1], 0, HALF)
+    take("zup", 32)
+    take("zdown", 96)
+    to_core(PLACE[3, 1], 0, 48)
     to_core(PLACE[1, 1], 0, HALF)
     forward(768, 128, 0, 512)
     forward(768, 128, 1024, 512)
@@ -261,15 +271,16 @@
     take("up2z", 32)
     take("down2z", 96)
     to_core(PLACE[2, 1], 0, BLOCK)
-    take("zup", 64)
+    take("zup", 48)
     take("zdown", 64)
-    to_core(PLACE[3, 1], 64, HALF)
+    take("zdown", 112)
+    to_core(PLACE[3, 1], 48, 80)
     to_core(PLACE[1, 1], 64, HALF)
     forward(512, 256, 0, 1024)
     forward(896, 128, 0, 512)
     forward(0, 512, 512, 512)
     forward(768, 256, 512, 512)
-    wait_core("7_0", "4_0", "5_0", "4_64", "5_64")
+    wait_core("7_0", "4_0", "5_0", "4_64", "5_48")
     forward(512, 256, 1024, 1024)
     forward(896, 128, 1024, 512)
     forward(0, 512, 1536, 512)
@@ -526,15 +537,15 @@
         total = total + sums_b[index]
     totals_ref[...] = total
     stores = []
-    for tree, source, result in ((image_tree, image_ref, sum_image_hbm), (text_tree, text_ref, sum_text_hbm)):
+    for tree, result in ((image_tree, sum_image_hbm), (text_tree, sum_text_hbm)):
         label, acc, out, landing, peer = tree
         for name in ("up_free", "down_free", "z_g0", "z_g64", "up_last0", "down_last0", "up_last32", "down_last32"):
             copies.arrived(label + name)
         grad = acc[block(0), :]
         for slot in (4, 5, 6):
             grad = grad + landing[block(slot), :].astype(F32)
-        source[...] = grad
-        stores.append(pltpu.make_async_copy(source, result, local_sems.at[2 + len(stores)]))
+        out[block(0), :] = grad.astype(BF16)
+        stores.append(pltpu.make_async_copy(out.at[block(0)], result, local_sems.at[2 + len(stores)]))
         stores[-1].start()
     copies.settle(len(copies.table))
     for store in stores:
@@ -560,7 +571,7 @@
     ):
         rows = source[...]
         inverse = lax.rsqrt(jnp.sum(rows * rows, axis=1, keepdims=True) + 1e-06)
-        grad = total[...] * scale
+        grad = total[...].astype(F32) * scale
         unit = rows * inverse
         result[...] = inverse * (grad - unit * jnp.sum(unit * grad, axis=1, keepdims=True))
     totals = totals_ref[...]
@@ -574,9 +585,10 @@
     anywhere = pl.BlockSpec(memory_space=pl.ANY)
     one = jax.ShapeDtypeStruct((1, 1), F32)
     shape = jax.ShapeDtypeStruct((BLOCK, WIDTH), F32)
+    low_shape = jax.ShapeDtypeStruct((BLOCK, WIDTH), BF16)
     totals, sum_image, sum_text = pl.pallas_call(
         kernel,
-        out_shape=(jax.ShapeDtypeStruct((8, 128), F32), shape, shape),
+        out_shape=(jax.ShapeDtypeStruct((8, 128), F32), low_shape, low_shape),
         in_specs=[smem, anywhere, anywhere],
         out_specs=(pl.BlockSpec(memory_space=pltpu.VMEM), anywhere, anywhere),
         scratch_shapes=[
@@ -606,8 +618,8 @@
             pltpu.VMEM((7 * BLOCK, WIDTH), BF16),
             pltpu.VMEM((7 * BLOCK, WIDTH), BF16),
             pltpu.VMEM((1024, WIDTH), BF16),
-            pltpu.SemaphoreType.DMA((160,)),
-            pltpu.SemaphoreType.DMA((160,)),
+            pltpu.SemaphoreType.DMA((168,)),
+            pltpu.SemaphoreType.DMA((168,)),
             pltpu.SemaphoreType.DMA((4,)),
         ],
         compiler_params=pltpu.CompilerParams(

time: 77.6 us -> 77.2 us (level)
  no operation moved by 1% of the time
where the time goes in v2:
time: 77.2 us; the launch traced here: 77 us
  Pallas kernels  75.7 us (98%)
  between operations  1.29 us (2%)
    pallas_call x1, Pallas kernels, on_device(): pl.pallas_call(kernel, out_shape=(jax.ShapeDtypeStruct((8, 128), F32), lo...  73.2 us
    pallas_call x1, Pallas kernels, on_device(): pl.pallas_call(finalize, grid=(BLOCK // step_rows,), out_shape=(one, shap...  2.58 us

profile of v2, /device:TPU:1, one launch (start us, length us, event | category | flops | bytes accessed | tf_op | source)
XLA Modules:
  0.0 77.0 jit_solution(9234892236887365039)
XLA Ops:
  1.3 73.2 %shard_map.66 = (f32[8,128]{1,0:T(8,128)}, bf16[128,1280]{1,0:T(8,128)(2,1)}, bf16[128,1280]{1,0:T(8,128)(2,1)}) custom-call(f32[1,1]{1,0:T(1,128)} %bitcast.3.temp_ref, f32[128,1280]{1,0:T(8,128)} %image_ref.1, f32[128,1280]{1,0:T(8,128)} %text_ref.1), custom_call_target="tpu_custom_call" | custom-call | flops 16106127360 | bytes 2621440 | tf_op jit(solution)/shard_map/pallas_call | solution.py:589
  74.4 2.6 %shard_map.67 = (f32[1,1]{1,0:T(1,128)}, f32[128,1280]{1,0:T(8,128)}, f32[128,1280]{1,0:T(8,128)}, f32[1,1]{1,0:T(1,128)}) custom-call(f32[1,1]{1,0:T(1,128)} %bitcast.4.temp_ref, f32[8,128]{1,0:T(8,128)} %get-tuple-element.11.totals_ref, f32[128,1280]{1,0:T(8,128)} %image_ref.1, f32[128,1280]{1,0:T(8,128)} %text_ref.1, ...), custom_call_target="tpu_custom_call" | custom-call | tf_op jit(solution)/shard_map/pallas_call | solution.py:632
